TPU v7x, 1024 devices: a whole 4x8x16 slice. The times are simulated.
1024 devices in a mesh: dp: 32 (over y_hi, z), mp: 32 (over x, y_lo, core).
Axes of the slice: x: 4, y: 8 (y_hi: 2, y_lo: 4; y = y_hi * 4 + y_lo), z: 16, core: 2. Of those that a mesh axis runs over, the one named last changes fastest.
Arguments:
- inputs: bfloat16 [16384, 3072], P(('dp', 'mp')), may hold values from -600 to 600
- gain: float32 [3072], replicated, may hold values from 0.1 to 1.9
- qkv_weight: bfloat16 [3072, 32, 384], P(None, 'mp'), may hold values from -0.5 to 0.5
- d_attended: bfloat16 [16384, 32, 128], P('dp', 'mp'), may hold values from -6 to 6
Outputs:
- attended: bfloat16 [16384, 32, 128], P('dp', 'mp')
- input_grad: bfloat16 [16384, 3072], P(('dp', 'mp'))
- weight_grad: float32 [3072, 32, 384], P('dp', 'mp')
All inputs are finite; a program needn't handle non-finite values.
Results may differ from a plain program's by a relative error of at most 0.04.
The roundings to bfloat16 on the way count: a program that leaves them out, or rounds other values in their place, can miss the bound.
Values may be sent and summed in bfloat16 or wider, within the bound.
A program may use at most 32 MiB of HBM per device.

v0:
```python
import jax
import jax.numpy as jnp
from jax import lax
from jax.sharding import PartitionSpec as P

PATCHES = 256


def normalize(rows, gain):
    mean = jnp.mean(rows, -1, keepdims=True)
    centered = rows - mean
    spread = jnp.mean(centered * centered, -1, keepdims=True)
    return centered * lax.rsqrt(spread + 1e-06) * gain


def attend(block, d_out):
    size = d_out.shape[-1]
    scale = size ** (-0.5)
    query = block[:, :size].astype(jnp.float32)
    keys = block[:, size : 2 * size].astype(jnp.float32)
    values = block[:, 2 * size :].astype(jnp.float32)
    scores = jnp.dot(query, keys.T) * scale
    peak = jnp.max(scores, -1, keepdims=True)
    expo = jnp.exp(scores - peak)
    probs = expo / jnp.sum(expo, -1, keepdims=True)
    probs_low = probs.astype(jnp.bfloat16).astype(jnp.float32)
    output = jnp.dot(probs_low, values).astype(jnp.bfloat16)
    d_outf = d_out.astype(jnp.float32)
    d_probs = jnp.dot(d_outf, values.T)
    d_values = jnp.dot(probs_low.T, d_outf)
    d_scores = (
        (probs * (d_probs - jnp.sum(d_probs * probs, -1, keepdims=True)) * scale)
        .astype(jnp.bfloat16)
        .astype(jnp.float32)
    )
    d_query = jnp.dot(d_scores, keys)
    d_keys = jnp.dot(d_scores.T, query)
    return (output, jnp.concatenate([d_query, d_keys, d_values], -1).astype(jnp.bfloat16))


def local(inputs, gain, qkv_weight, d_attended):
    rows, width = inputs.shape
    group_rows, heads, size = d_attended.shape
    weight = qkv_weight.reshape(width, heads * 3 * size)
    normed32, back = jax.vjp(lambda r: normalize(r, gain), inputs.astype(jnp.float32))
    normed = normed32.astype(jnp.bfloat16)
    qkv = jnp.dot(
        lax.all_gather(normed, "mp", axis=0, tiled=True), weight, preferred_element_type=jnp.float32
    ).astype(jnp.bfloat16)
    images = group_rows // PATCHES
    per_image = jax.vmap(jax.vmap(attend, in_axes=(1, 1), out_axes=(1, 1)))
    output, d_qkv = per_image(
        qkv.reshape(images, PATCHES, heads, 3 * size),
        d_attended.reshape(images, PATCHES, heads, size),
    )
    attended = output.reshape(group_rows, heads, size)
    d_flat = d_qkv.reshape(group_rows, heads * 3 * size)
    part = d_flat
    grad_local = lax.dot_general(
        lax.all_gather(normed, "mp", axis=0, tiled=True),
        part,
        (((0,), (0,)), ((), ())),
        preferred_element_type=jnp.float32,
    )
    part = d_flat
    d_normed = lax.psum_scatter(
        lax.dot_general(
            part, weight, (((1,), (1,)), ((), ())), preferred_element_type=jnp.float32
        ).astype(jnp.bfloat16),
        "mp",
        scatter_dimension=0,
        tiled=True,
    ).astype(jnp.float32)
    input_grad = back(d_normed)[0].astype(jnp.bfloat16)
    summed = lax.psum_scatter(
        grad_local.astype(jnp.bfloat16), "dp", scatter_dimension=0, tiled=True
    ).astype(jnp.float32)
    weight_grad = summed.reshape(summed.shape[0], heads, 3 * size)
    return (attended, input_grad, weight_grad)


def solution(mesh):
    return jax.shard_map(
        local,
        mesh=mesh,
        in_specs=(P(("dp", "mp"), None), P(), P(None, "mp", None), P("dp", "mp", None)),
        out_specs=(P("dp", "mp", None), P(("dp", "mp"), None), P("dp", "mp", None)),
        check_vma=False,
    )
```

profile of v0, /device:TPU:64, one launch (start us, length us, event | category | flops | bytes accessed | tf_op | source)
XLA Modules:
  0.0 966.7 jit_solution(14786550731055306424)
XLA Ops:
  7.2 0.0 copy-start
  7.2 0.0 all-gather.2.cloned.1.call-start
  7.2 1.2 convert_reduce_fusion
  8.4 1.1 fusion.24
  9.5 1.6 fusion.26
  11.2 0.0 all-gather.2.cloned.1.call-update
  11.2 0.0 copy-start.3
  11.2 0.0 reduce-scatter.5.cloned.1.call-start
  11.2 76.6 %all-gather.2.cloned.1.call-done = bf16[512,3072]{1,0:T(8,128)(2,1)} async-done(((bf16[16,3072]{1,0:T(8,128)(2,1)}), bf16[512,3072]{1,0:T(8,128)(2,1)}) %all-gather.2.cloned.1.call-update) | async-done | bytes 3145744 | tf_op jit(solution)/shard_map/all_gather | solution.py:48
  87.8 0.0 copy-done
  87.8 3.7 fusion.6
  91.5 1.1 fusion.60
  92.6 0.0 copy-done.3
  92.6 0.2 convolution_bitcast_fusion
  92.8 1.6 convolution_convert_fusion.4
  94.5 2.2 convolution_convert_fusion.3
  96.7 0.5 convolution_convert_fusion.2
  97.2 0.0 copy-start.4
  97.2 5.2 convolution_convert_fusion.1
  102.4 0.0 reduce-scatter.5.cloned.1.call-update
  102.4 0.0 reduce-scatter.3.cloned.1.call-start
  102.5 0.0 copy-done.4
  102.5 3.5 convolution_convert_fusion
  106.0 0.0 copy-start.1
  106.0 0.0 copy-start.2
  106.0 0.0 reduce-scatter.3.cloned.1.call-update
  106.0 1.2 convolution_convert_fusion.5
  107.3 693.4 %reduce-scatter.5.cloned.1.call-done = bf16[96,384]{1,0:T(8,128)(2,1)} async-done(((bf16[3072,384]{1,0:T(8,128)(2,1)}), bf16[96,384]{1,0:T(8,128)(2,1)}) %reduce-scatter.5.cloned.1.call-update) | async-done | bytes 73744 | tf_op jit(solution)/shard_map/reduce_scatter | solution.py:75
  800.7 0.9 bitcast_convert_fusion
  801.6 0.8 copy.9
  802.4 153.9 %reduce-scatter.3.cloned.1.call-done = bf16[16,3072]{1,0:T(8,128)(2,1)} async-done(((bf16[512,3072]{1,0:T(8,128)(2,1)}), bf16[16,3072]{1,0:T(8,128)(2,1)}) %reduce-scatter.3.cloned.1.call-update) | async-done | bytes 98320 | tf_op jit(solution)/shard_map/reduce_scatter | solution.py:66
  956.3 0.0 copy-done.1
  956.3 0.0 copy-done.2
  956.3 1.1 fusion.27
  957.4 1.1 fusion.34
  958.5 1.7 add_convert_fusion
  (4 shorter events, 0.0 us)
Async XLA Ops:
  7.2 80.7 %copy-start = (bf16[3072,1,384]{2,0,1:T(8,128)(2,1)S(1)}, bf16[3072,1,384]{2,0,1:T(8,128)(2,1)}, u32[]{:S(2)}) copy-start(bf16[3072,1,384]{2,0,1:T(8,128)(2,1)} %param.6) | copy-start | bytes 7077892
  7.2 80.6 %all-gather.2.cloned.1.call-start = ((), (), s32[]{:S(2)}) async-start(), calls=%async_computation.2 | async-start | bytes 3244032 | tf_op jit(solution)/shard_map/all_gather | solution.py:48
  11.2 81.4 %copy-start.3 = (bf16[512,1,128]{2,0,1:T(8,128)(2,1)S(1)}, bf16[512,1,128]{2,0,1:T(8,128)(2,1)}, u32[]{:S(2)}) copy-start(bf16[512,1,128]{2,0,1:T(8,128)(2,1)} %param.7) | copy-start | bytes 393220
  11.2 789.5 %reduce-scatter.5.cloned.1.call-start = ((), (), s32[]{:S(2)}) async-start(), calls=%async_computation.4 | async-start | bytes 2433024 | tf_op jit(solution)/shard_map/reduce_scatter | solution.py:75
  97.2 5.3 copy-start.4
  102.4 853.8 %reduce-scatter.3.cloned.1.call-start = ((), (), s32[]{:S(2)}) async-start(), calls=%async_computation.3 | async-start | bytes 3244032 | tf_op jit(solution)/shard_map/reduce_scatter | solution.py:66
  106.0 850.3 %copy-start.1 = (bf16[16,3072]{1,0:T(8,128)(2,1)S(1)}, bf16[16,3072]{1,0:T(8,128)(2,1)}, u32[]{:S(2)}) copy-start(bf16[16,3072]{1,0:T(8,128)(2,1)} %param.4) | copy-start | bytes 294916
  106.0 850.3 %copy-start.2 = (f32[3072]{0:T(1024)S(1)}, f32[3072]{0:T(1024)}, u32[]{:S(2)}) copy-start(f32[3072]{0:T(1024)} %param.5) | copy-start | bytes 36868
Sparse Core Ops, SparseCore 0:
  11.3 76.4 all-gather.1
  102.6 698.0 reduce-scatter.4
  804.5 151.7 reduce-scatter.2
where the time goes:
time: 967 us
  waiting for transfers between devices  924 us (96%)
  matrix products  19.3 us (2%)
  between operations  13.8 us (1%)
    reduce_scatter x1, waiting for transfers between devices, local(): lax.psum_scatter(grad_local.astype(jnp.bfloat16), 'dp', scatter_dimension...  693 us
    reduce_scatter x1, waiting for transfers between devices, local(): lax.psum_scatter(lax.dot_general(part, weight, (((1,), (1,)), ((), ())),...  154 us
    all_gather x1, waiting for transfers between devices, local(): lax.all_gather(normed, 'mp', axis=0, tiled=True)  76.6 us
  transfers between devices with their start and end apart: 3, of which 3 were waited for; matrix products, arithmetic and copies ran while one was open for 1% of the time, Pallas kernels for 0%

commit v1 on v0

v1 whole, which is shorter than its diff:
```python
import jax
import jax.numpy as jnp
from jax import lax
from jax.experimental import pallas as pl
from jax.experimental.pallas import tpu as pltpu
from jax.sharding import PartitionSpec as P

MESH = pl.DeviceIdType.MESH
BF16, F32 = jnp.bfloat16, jnp.float32

NX, NY, NC, NZ, NH = 4, 4, 2, 16, 2
ROWS, D, HD = 16, 3072, 128
QKV = 3 * HD
GROUP = NX * NY * NC * ROWS
IMAGE = GROUP // 2
HALF = D // 2
OWN = D // (NZ * NH)
RIGHT_STEPS, LEFT_STEPS = NZ // 2, NZ // 2 - 1
TILE = 4 * OWN


def mod(a, n):
    return lax.rem(a, jnp.int32(n))


def div(a, n):
    return lax.div(a, jnp.int32(n))


def dot(a, b, ca, cb):
    return lax.dot_general(a, b, (((ca,), (cb,)), ((), ())), preferred_element_type=F32)


def arrived(ref, sem):
    pltpu.make_async_copy(ref, ref, sem).wait()


def kernel(
    in_ref, gain_ref, w_hbm, do_hbm,
    att_ref, ing_ref, wg_ref,
    w, do, normed, qkv, dqkv, grads, terms, from_core, half_l, half_r, full_l, full_r, from_y,
    zin_r, zin_l, yh_out, yh_in,
    sem_w, sem_do, sem_y, sem_xl, sem_xr, sem_x2l, sem_x2r, sem_sib,
    sem_zr, sem_zl, sem_core, sem_hl, sem_hr, sem_fl, sem_fr, sem_fy, sem_yh,
    out_ag, out_z, out_mp, out_yh,
):
    dp, mp = lax.axis_index("dp"), lax.axis_index("mp")
    x, y, c = div(mp, 8), mod(div(mp, 2), 4), mod(mp, 2)
    h, z = div(dp, NZ), mod(dp, NZ)
    xr, xl, xo = mod(x + 1, NX), mod(x + 3, NX), mod(x + 2, NX)
    other_c, other_h = 1 - c, 1 - h
    near = [y, y + 1 - 2 * mod(y, 2), mod(y + 2, NY), NY - 1 - y]

    def at_mp(xx, yy, cc):
        return (dp, xx * 8 + yy * 2 + cc)

    to_right, to_left = at_mp(xr, y, c), at_mp(xl, y, c)
    to_sib = at_mp(x, y, other_c)
    to_zr, to_zl = (h * NZ + mod(z + 1, NZ), mp), (h * NZ + mod(z + NZ - 1, NZ), mp)
    to_yh = (other_h * NZ + z, mp)

    def send(src, dst, out_sem, in_sem, device):
        pltpu.make_async_remote_copy(
            src_ref=src, dst_ref=dst, send_sem=out_sem, recv_sem=in_sem, device_id=device, device_id_type=MESH
        ).start()

    barrier = pltpu.get_barrier_semaphore()
    partners = [to_right, to_left, to_sib, to_zr, to_zl, to_yh] + [at_mp(x, near[k], c) for k in (1, 2, 3)]
    for device in partners:
        pl.semaphore_signal(barrier, inc=1, device_id=device, device_id_type=MESH)
    load_w = pltpu.make_async_copy(w_hbm, w, sem_w)
    load_w.start()
    load_do = pltpu.make_async_copy(do_hbm, do, sem_do)
    load_do.start()

    rows = in_ref[...].astype(F32)
    gain = gain_ref[...]
    mean = jnp.sum(rows, -1, keepdims=True) * (1.0 / D)
    centered = rows - mean
    inv = lax.rsqrt(jnp.sum(centered * centered, -1, keepdims=True) * (1.0 / D) + 1e-6)
    normed[x, y, c] = (centered * inv * gain).astype(BF16)

    pl.semaphore_wait(barrier, len(partners))

    def to_sibling(ref, slot):
        send(ref, ref, out_ag, sem_sib.at[slot], to_sib)

    def along_x(yy):
        block = normed.at[x, yy, c]
        send(block, block, out_ag, sem_xl.at[yy], to_right)
        send(block, block, out_ag, sem_xr.at[yy], to_left)

    own = normed.at[x, y, c]
    along_x(y)
    for k in (1, 2, 3):
        send(own, own, out_ag, sem_y.at[y], at_mp(x, near[k], c))
    to_sibling(own, 0)
    for k in range(NY):
        if k + 1 < NY:
            yy = near[k + 1]
            arrived(normed.at[x, yy, c], sem_y.at[yy])
            along_x(yy)
            to_sibling(normed.at[x, yy, c], 0)
        yy = near[k]
        block = normed.at[xl, yy, c]
        arrived(block, sem_xl.at[yy])
        piece = block.at[:, pl.ds(0, HALF)]
        send(piece, piece, out_ag, sem_x2l.at[yy], to_right)
        to_sibling(block, 1)
        block = normed.at[xr, yy, c]
        arrived(block, sem_xr.at[yy])
        piece = block.at[:, pl.ds(HALF, HALF)]
        send(piece, piece, out_ag, sem_x2r.at[yy], to_left)
        to_sibling(block, 2)

    def project(xx):
        qkv[xx] = dot(normed[xx].reshape(IMAGE // 2, D), w[...], 1, 0).astype(BF16)

    def second(k):
        yy = near[k]
        piece = normed.at[xo, yy, c, :, pl.ds(0, HALF)]
        arrived(piece, sem_x2l.at[yy])
        to_sibling(piece, 3)
        piece = normed.at[xo, yy, c, :, pl.ds(HALF, HALF)]
        arrived(piece, sem_x2r.at[yy])
        to_sibling(piece, 3)

    def bundle(xx, slot):
        arrived(normed.at[xx, :, other_c], sem_sib.at[slot])

    def attend(a):
        block = qkv[pl.ds(2 * a, 2)].reshape(IMAGE, QKV)
        q, k, v = block[:, :HD], block[:, HD : 2 * HD], block[:, 2 * HD :]
        d_out = do[a]
        scale = HD ** (-0.5)
        scores = dot(q, k, 1, 1) * scale
        expo = jnp.exp(scores - jnp.max(scores, -1, keepdims=True))
        probs = expo / jnp.sum(expo, -1, keepdims=True)
        low = probs.astype(BF16)
        att_ref[a] = dot(low, v, 1, 0).astype(BF16)
        d_probs = dot(d_out, v, 1, 1)
        dqkv[a, :, 2 * HD :] = dot(low, d_out, 0, 0).astype(BF16)
        d_scores = (probs * (d_probs - jnp.sum(d_probs * probs, -1, keepdims=True)) * scale).astype(BF16)
        dqkv[a, :, :HD] = dot(d_scores, k, 1, 0).astype(BF16)
        dqkv[a, :, HD : 2 * HD] = dot(d_scores, q, 0, 0).astype(BF16)

    load_w.wait()
    load_do.wait()
    bundle(x, 0)
    project(x)
    second(0)
    second(1)
    bundle(xl, 1)
    bundle(xr, 2)
    image = div(x, 2)
    mate = x + 1 - 2 * mod(x, 2)
    project(mate)
    second(2)
    second(3)
    attend(image)
    project(mod(mate + 2, NX))
    bundle(xo, 3)
    project(xo)
    attend(1 - image)

    def grad_tile(t):
        u = mod(t, 4)
        d_all = dqkv[...].reshape(GROUP, QKV)
        for hh in range(NH):
            cols = pl.ds(pl.multiple_of((u + 4 * hh) * TILE, 128), TILE)
            tile = normed[:, :, :, :, cols].reshape(GROUP, TILE)
            grads[hh, pl.ds(4 * u, 4)] = dot(tile, d_all, 0, 0).astype(BF16).reshape(4, OWN, QKV)

    subs = (other_h, h)

    def z_right(s):
        zz = mod(z + 8 - s + NZ, NZ)
        for sub in range(2):
            block = grads.at[subs[sub], zz]
            if s > 0:
                arrived(zin_r.at[s - 1, sub], sem_zr.at[s - 1, sub])
                block[...] = (block[...].astype(F32) + zin_r[s - 1, sub].astype(F32)).astype(BF16)
            send(block, zin_r.at[s, sub], out_z, sem_zr.at[s, sub], to_zr)

    def z_left(s):
        zz = mod(z + 9 + s, NZ)
        for sub in range(2):
            block = grads.at[subs[sub], zz]
            if s > 0:
                arrived(zin_l.at[s - 1, sub], sem_zl.at[s - 1, sub])
                block[...] = (block[...].astype(F32) + zin_l[s - 1, sub].astype(F32)).astype(BF16)
            send(block, zin_l.at[s, sub], out_z, sem_zl.at[s, sub], to_zl)

    def z_step(s):
        z_right(s)
        if s < LEFT_STEPS:
            z_left(s)

    first = div(mod(z + 8, NZ), 4)
    grad_tile(first)
    grad_tile(first + 1)
    z_step(0)
    grad_tile(first + 3)
    grad_tile(first + 2)

    def share(j, carry):
        cols = pl.ds(pl.multiple_of(j * 256, 256), 256)
        out = dot(dqkv[...].reshape(GROUP, QKV), w[cols, :], 1, 1).astype(BF16)
        terms[:, :, :, :, cols] = out.reshape(NX, NY, NC, ROWS, 256)
        return carry

    lax.fori_loop(0, D // 256, share, 0)
    order = (xo, xr, xl, x)
    for j in range(NX):
        send(terms.at[order[j], :, other_c], from_core.at[j], out_mp, sem_core.at[j], to_sib)
    z_step(1)

    ys = [mod(y + 1, NY), mod(y + 2, NY), mod(y + 3, NY), y]

    def both_cores(j, k):
        return terms[order[j], ys[k], c].astype(F32) + from_core[j, ys[k]].astype(F32)

    def start_x(k):
        block = terms.at[xo, ys[k], c]
        block[...] = both_cores(0, k).astype(BF16)
        send(block.at[:, pl.ds(0, HALF)], half_l.at[k], out_mp, sem_hl.at[k], to_right)
        send(block.at[:, pl.ds(HALF, HALF)], half_r.at[k], out_mp, sem_hr.at[k], to_left)

    def relay_x(k):
        total = both_cores(1, k)
        block = terms.at[xr, ys[k], c]
        arrived(half_l.at[k], sem_hl.at[k])
        block[:, :HALF] = (total[:, :HALF] + half_l[k].astype(F32)).astype(BF16)
        block[:, HALF:] = total[:, HALF:].astype(BF16)
        send(block, full_l.at[k], out_mp, sem_fl.at[k], to_right)
        total = both_cores(2, k)
        block = terms.at[xl, ys[k], c]
        arrived(half_r.at[k], sem_hr.at[k])
        block[:, :HALF] = total[:, :HALF].astype(BF16)
        block[:, HALF:] = (total[:, HALF:] + half_r[k].astype(F32)).astype(BF16)
        send(block, full_r.at[k], out_mp, sem_fr.at[k], to_left)

    def end_x(k):
        total = both_cores(3, k)
        arrived(full_l.at[k], sem_fl.at[k])
        arrived(full_r.at[k], sem_fr.at[k])
        total = total + full_l[k].astype(F32) + full_r[k].astype(F32)
        if k == NY - 1:
            return total
        block = terms.at[x, ys[k], c]
        block[...] = total.astype(BF16)
        send(block, from_y.at[y], out_mp, sem_fy.at[y], at_mp(x, ys[k], c))
        return None

    arrived(from_core.at[0], sem_core.at[0])
    for k in range(NY):
        start_x(k)
    z_step(2)
    arrived(from_core.at[1], sem_core.at[1])
    arrived(from_core.at[2], sem_core.at[2])
    relay_x(0)
    relay_x(1)
    z_step(3)
    relay_x(2)
    relay_x(3)
    z_step(4)
    arrived(from_core.at[3], sem_core.at[3])
    end_x(0)
    end_x(1)
    z_step(5)
    end_x(2)
    d_normed = end_x(3)
    z_step(6)
    for k in range(NY - 1):
        arrived(from_y.at[ys[k]], sem_fy.at[ys[k]])
        d_normed = d_normed + from_y[ys[k]].astype(F32)
    rows = in_ref[...].astype(F32)
    centered = rows - jnp.sum(rows, -1, keepdims=True) * (1.0 / D)
    inv = lax.rsqrt(jnp.sum(centered * centered, -1, keepdims=True) * (1.0 / D) + 1e-6)
    hat = centered * inv
    grown = d_normed * gain_ref[...]
    lean = jnp.sum(grown * hat, -1, keepdims=True) * (1.0 / D)
    ing_ref[...] = (inv * (grown - jnp.sum(grown, -1, keepdims=True) * (1.0 / D) - hat * lean)).astype(BF16)
    z_step(7)

    def z_end(sub):
        arrived(zin_l.at[LEFT_STEPS - 1, sub], sem_zl.at[LEFT_STEPS - 1, sub])
        arrived(zin_r.at[RIGHT_STEPS - 1, sub], sem_zr.at[RIGHT_STEPS - 1, sub])
        return (
            grads[subs[sub], z].astype(F32)
            + zin_l[LEFT_STEPS - 1, sub].astype(F32)
            + zin_r[RIGHT_STEPS - 1, sub].astype(F32)
        )

    yh_out[...] = z_end(0).astype(BF16)
    send(yh_out, yh_in, out_yh, sem_yh, to_yh)
    total = z_end(1)
    arrived(yh_in, sem_yh)
    wg_ref[...] = total + yh_in[...].astype(F32)

    blocks = NX * NY * NC - 1
    for sem in (out_ag, out_mp):
        pltpu.make_async_copy(
            normed.at[pl.ds(0, 3)], normed.at[pl.ds(0, 3)], sem
        ).wait()
        pltpu.make_async_copy(normed.at[3, pl.ds(0, 3)], normed.at[3, pl.ds(0, 3)], sem).wait()
        pltpu.make_async_copy(normed.at[3, 3, 0], normed.at[3, 3, 0], sem).wait()
    assert blocks == 31
    pltpu.make_async_copy(grads.at[0], grads.at[0], out_z).wait()
    pltpu.make_async_copy(grads.at[1, pl.ds(0, 14)], grads.at[1, pl.ds(0, 14)], out_z).wait()
    pltpu.make_async_copy(yh_out, yh_out, out_yh).wait()


def local(inputs, gain, qkv_weight, d_attended):
    vmem, anywhere = pl.BlockSpec(memory_space=pltpu.VMEM), pl.BlockSpec(memory_space=pl.ANY)
    dma = pltpu.SemaphoreType.DMA
    blocks = (NX, NY, NC, ROWS, D)
    attended, input_grad, weight_grad = pl.pallas_call(
        kernel,
        out_shape=(
            jax.ShapeDtypeStruct((2, IMAGE, HD), BF16),
            jax.ShapeDtypeStruct((ROWS, D), BF16),
            jax.ShapeDtypeStruct((OWN, QKV), F32),
        ),
        in_specs=[vmem, vmem, anywhere, anywhere],
        out_specs=(vmem, vmem, vmem),
        scratch_shapes=[
            pltpu.VMEM((D, QKV), BF16),
            pltpu.VMEM((2, IMAGE, HD), BF16),
            pltpu.VMEM(blocks, BF16),
            pltpu.VMEM((NX, IMAGE // 2, QKV), BF16),
            pltpu.VMEM((2, IMAGE, QKV), BF16),
            pltpu.VMEM((NH, NZ, OWN, QKV), BF16),
            pltpu.VMEM(blocks, BF16),
            pltpu.VMEM((NX, NY, ROWS, D), BF16),
            pltpu.VMEM((NY, ROWS, HALF), BF16),
            pltpu.VMEM((NY, ROWS, HALF), BF16),
            pltpu.VMEM((NY, ROWS, D), BF16),
            pltpu.VMEM((NY, ROWS, D), BF16),
            pltpu.VMEM((NY, ROWS, D), BF16),
            pltpu.VMEM((RIGHT_STEPS, 2, OWN, QKV), BF16),
            pltpu.VMEM((LEFT_STEPS, 2, OWN, QKV), BF16),
            pltpu.VMEM((OWN, QKV), BF16),
            pltpu.VMEM((OWN, QKV), BF16),
            dma, dma,
            dma((NY,)), dma((NY,)), dma((NY,)), dma((NY,)), dma((NY,)), dma((4,)),
            dma((RIGHT_STEPS, 2)), dma((LEFT_STEPS, 2)),
            dma((NX,)), dma((NY,)), dma((NY,)), dma((NY,)), dma((NY,)), dma((NY,)), dma,
            dma, dma, dma, dma,
        ],
        compiler_params=pltpu.CompilerParams(
            collective_id=0, has_side_effects=True, vmem_limit_bytes=48 * 1024 * 1024
        ),
    )(inputs, gain.reshape(1, D), qkv_weight.reshape(D, QKV), d_attended.reshape(2, IMAGE, HD))
    return (attended.reshape(GROUP, 1, HD), input_grad, weight_grad.reshape(OWN, 1, QKV))


def solution(mesh):
    return jax.shard_map(
        local,
        mesh=mesh,
        in_specs=(P(("dp", "mp"), None), P(), P(None, "mp", None), P("dp", "mp", None)),
        out_specs=(P("dp", "mp", None), P(("dp", "mp"), None), P("dp", "mp", None)),
        check_vma=False,
    )
```

time: 967 us -> 91.6 us (0.09)
  the two profiles are of different devices: /device:TPU:64 before, /device:TPU:56 now
where the time goes in v1:
time: 91.6 us; the launch traced here: 91.3 us
  Pallas kernels  84.4 us (92%)
  local copies, waits for them, and re-layouts  6.27 us (7%)
    pallas_call x1, Pallas kernels, local(): pl.pallas_call(kernel, out_shape=(jax.ShapeDtypeStruct((2, IMAGE, HD), BF...  84.4 us
    unnamed x11, local copies, waits for them, and re-layouts  6.27 us

profile of v1, /device:TPU:56, one launch (start us, length us, event | category | flops | bytes accessed | tf_op | source)
XLA Modules:
  0.0 91.3 jit_solution(5460833408154414406)
XLA Ops:
  0.6 0.0 copy-start
  0.6 1.7 %copy-done = bf16[3072,1,384]{2,0,1:T(8,128)(2,1)S(1)} copy-done((bf16[3072,1,384]{2,0,1:T(8,128)(2,1)S(1)}, bf16[3072,1,384]{2,0,1:T(8,128)(2,1)}, u32[]{:S(2)}) %copy-start) | copy-done | bytes 2359320
  2.3 0.0 copy-start.1
  2.3 0.9 copy-done.1
  3.2 0.0 copy-start.2
  3.2 0.9 copy-done.2
  4.1 0.0 copy-start.3
  4.1 0.7 copy-done.3
  4.8 84.4 %shard_map.67 = (bf16[2,256,128]{2,1,0:T(8,128)(2,1)S(1)}, bf16[16,3072]{1,0:T(8,128)(2,1)S(1)}, f32[96,384]{1,0:T(8,128)S(1)}) custom-call(bf16[16,3072]{1,0:T(8,128)(2,1)S(1)} %copy-done.2, f32[1,3072]{1,0:T(1,128)S(1)} %bitcast.9, bf16[3072,384]{1,0:T(8,128)(2,1)S(1)} %bitcast.5, bf16[2,256,128]{2,1,0:T(8,128)(2,1)S(1)} %bitcast.7), custom_call_target="tpu_custom_call" | custom-call | tf_op jit(solution)/shard_map/pallas_call | solution.py:318
  89.2 0.8 copy.7
  90.0 0.7 copy.10
  90.7 0.6 copy.11
Async XLA Ops:
  0.6 1.7 %copy-start = (bf16[3072,1,384]{2,0,1:T(8,128)(2,1)S(1)}, bf16[3072,1,384]{2,0,1:T(8,128)(2,1)}, u32[]{:S(2)}) copy-start(bf16[3072,1,384]{2,0,1:T(8,128)(2,1)} %param.6) | copy-start | bytes 7077892
  2.3 0.9 copy-start.1
  3.2 0.9 copy-start.2
  4.1 0.7 copy-start.3

commit v2 on v1

v2 whole, which is shorter than its diff:
```python
import jax
import jax.numpy as jnp
from jax import lax
from jax.experimental import pallas as pl
from jax.experimental.pallas import tpu as pltpu
from jax.sharding import PartitionSpec as P

MESH = pl.DeviceIdType.MESH
STRAIGHT = (True, False, False, True)
Y_FIRST = (1, 2, 3)
Z_PARTS = 2
BF16, F32 = jnp.bfloat16, jnp.float32

NX, NY, NC, NZ, NH = 4, 4, 2, 16, 2
ROWS, D, HD = 16, 3072, 128
QKV = 3 * HD
GROUP = NX * NY * NC * ROWS
IMAGE = GROUP // 2
HALF = D // 2
OWN = D // (NZ * NH)
RIGHT_STEPS, LEFT_STEPS = NZ // 2, NZ // 2 - 1
PART = OWN // Z_PARTS
TILE = 4 * OWN


def mod(a, n):
    return lax.rem(a, jnp.int32(n))


def div(a, n):
    return lax.div(a, jnp.int32(n))


def dot(a, b, ca, cb):
    return lax.dot_general(a, b, (((ca,), (cb,)), ((), ())), preferred_element_type=F32)


def arrived(ref, sem):
    pltpu.make_async_copy(ref, ref, sem).wait()


def kernel(
    in_hbm, gain_hbm, w_hbm, do_hbm,
    att_hbm, ing_hbm, wg_hbm,
    att_ref, ing_ref, wg_ref,
    in_ref, gain_ref, w, do, normed, qkv, dqkv, grads, terms, from_core, half_l, half_r, full_l, full_r, from_y,
    zin_r, zin_l, yh_in,
    sem_in, sem_gain, sem_w, sem_do, sem_y, sem_xl, sem_xr, sem_xo, sem_x2l, sem_x2r, sem_sib,
    sem_zr, sem_zl, sem_core, sem_hl, sem_hr, sem_fl, sem_fr, sem_fy, sem_yh, sem_own, sem_att, sem_ing, sem_wg,
    out_ag, out_z, out_mp,
):
    dp, mp = lax.axis_index("dp"), lax.axis_index("mp")
    x, y, c = div(mp, 8), mod(div(mp, 2), 4), mod(mp, 2)
    h, z = div(dp, NZ), mod(dp, NZ)
    xr, xl, xo = mod(x + 1, NX), mod(x + 3, NX), mod(x + 2, NX)
    other_c, other_h = 1 - c, 1 - h
    near = [y, y + 1 - 2 * mod(y, 2), mod(y + 2, NY), NY - 1 - y]

    def at_mp(xx, yy, cc):
        return (dp, xx * 8 + yy * 2 + cc)

    to_right, to_left = at_mp(xr, y, c), at_mp(xl, y, c)
    to_sib, to_across = at_mp(x, y, other_c), at_mp(xo, y, c)
    to_zr, to_zl = (h * NZ + mod(z + 1, NZ), mp), (h * NZ + mod(z + NZ - 1, NZ), mp)
    over, over_zr, over_zl = ((other_h * NZ + mod(z + step, NZ), mp) for step in (0, 1, NZ - 1))

    def send(src, dst, out_sem, in_sem, device):
        pltpu.make_async_remote_copy(
            src_ref=src, dst_ref=dst, send_sem=out_sem, recv_sem=in_sem, device_id=device, device_id_type=MESH
        ).start()

    barrier = pltpu.get_barrier_semaphore()
    partners = [to_right, to_left, to_across, to_sib, to_zr, to_zl, over, over_zr, over_zl] + [at_mp(x, near[k], c) for k in (1, 2, 3)]
    for device in partners:
        pl.semaphore_signal(barrier, inc=1, device_id=device, device_id_type=MESH)
    load_in = pltpu.make_async_copy(in_hbm, in_ref, sem_in)
    load_in.start()
    load_gain = pltpu.make_async_copy(gain_hbm, gain_ref, sem_gain)
    load_gain.start()
    load_w = pltpu.make_async_copy(w_hbm, w, sem_w)
    load_w.start()
    load_do = pltpu.make_async_copy(do_hbm, do, sem_do)
    load_do.start()

    load_in.wait()
    load_gain.wait()
    rows = in_ref[...].astype(F32)
    gain = gain_ref[...]
    mean = jnp.sum(rows, -1, keepdims=True) * (1.0 / D)
    centered = rows - mean
    inv = lax.rsqrt(jnp.sum(centered * centered, -1, keepdims=True) * (1.0 / D) + 1e-6)
    normed[x, y, c] = (centered * inv * gain).astype(BF16)

    pl.semaphore_wait(barrier, len(partners))

    def to_sibling(ref, slot):
        send(ref, ref, out_ag, sem_sib.at[slot], to_sib)

    pieces = (pl.ds(0, HALF), pl.ds(HALF, HALF))

    def along_x(k):
        yy = near[k]
        block = normed.at[x, yy, c]
        for right, p in ((True, 0), (False, 1), (True, 1), (False, 0)):
            part = block.at[:, pieces[p]]
            sem, device = (sem_xl, to_right) if right else (sem_xr, to_left)
            send(part, part, out_ag, sem.at[yy, p], device)
        if STRAIGHT[k]:
            send(block, block, out_ag, sem_xo.at[yy], to_across)

    def along_y(k):
        send(own, own, out_ag, sem_y.at[y], at_mp(x, near[k], c))

    def pass_on(k):
        yy = near[k]
        if not STRAIGHT[k]:
            part = normed.at[xl, yy, c, :, pieces[0]]
            arrived(part, sem_xl.at[yy, 0])
            send(part, part, out_ag, sem_x2l.at[yy], to_right)
            part = normed.at[xr, yy, c, :, pieces[1]]
            arrived(part, sem_xr.at[yy, 1])
            send(part, part, out_ag, sem_x2r.at[yy], to_left)

    def finish_x(k):
        yy = near[k]
        if STRAIGHT[k]:
            arrived(normed.at[xl, yy, c, :, pieces[0]], sem_xl.at[yy, 0])
            arrived(normed.at[xr, yy, c, :, pieces[1]], sem_xr.at[yy, 1])
        arrived(normed.at[xl, yy, c, :, pieces[1]], sem_xl.at[yy, 1])
        to_sibling(normed.at[xl, yy, c], 1)
        arrived(normed.at[xr, yy, c, :, pieces[0]], sem_xr.at[yy, 0])
        to_sibling(normed.at[xr, yy, c], 2)

    own = normed.at[x, y, c]
    along_x(0)
    for k in Y_FIRST:
        along_y(k)
    to_sibling(own, 0)
    for k in range(NY):
        if k + 1 < NY:
            yy = near[k + 1]
            arrived(normed.at[x, yy, c], sem_y.at[yy])
            along_x(k + 1)
            to_sibling(normed.at[x, yy, c], 0)
        if k == 0:
            for j in (1, 2, 3):
                if j not in Y_FIRST:
                    along_y(j)
        pass_on(k)
        if k > 0:
            finish_x(k - 1)
    finish_x(NY - 1)

    def second(k):
        yy = near[k]
        if STRAIGHT[k]:
            block = normed.at[xo, yy, c]
            arrived(block, sem_xo.at[yy])
            to_sibling(block, 3)
            return
        for p, sem in ((0, sem_x2l), (1, sem_x2r)):
            part = normed.at[xo, yy, c, :, pieces[p]]
            arrived(part, sem.at[yy])
            to_sibling(part, 3)

    def bundle(xx, slot):
        arrived(normed.at[xx, :, other_c], sem_sib.at[slot])

    def project(xx):
        qkv[xx] = dot(normed[xx].reshape(IMAGE // 2, D), w[...], 1, 0).astype(BF16)

    def attend(a):
        block = qkv[pl.ds(2 * a, 2)].reshape(IMAGE, QKV)
        q, k, v = block[:, :HD], block[:, HD : 2 * HD], block[:, 2 * HD :]
        d_out = do[a]
        scale = HD ** (-0.5)
        scores = dot(q, k, 1, 1) * scale
        expo = jnp.exp(scores - jnp.max(scores, -1, keepdims=True))
        probs = expo / jnp.sum(expo, -1, keepdims=True)
        low = probs.astype(BF16)
        att_ref[a] = dot(low, v, 1, 0).astype(BF16)
        d_probs = dot(d_out, v, 1, 1)
        dqkv[a, :, 2 * HD :] = dot(low, d_out, 0, 0).astype(BF16)
        d_scores = (probs * (d_probs - jnp.sum(d_probs * probs, -1, keepdims=True)) * scale).astype(BF16)
        dqkv[a, :, :HD] = dot(d_scores, k, 1, 0).astype(BF16)
        dqkv[a, :, HD : 2 * HD] = dot(d_scores, q, 0, 0).astype(BF16)

    load_w.wait()
    load_do.wait()
    bundle(x, 0)
    project(x)
    second(0)
    second(1)
    bundle(xl, 1)
    bundle(xr, 2)
    image = div(x, 2)
    mate = x + 1 - 2 * mod(x, 2)
    project(mate)
    second(2)
    second(3)
    attend(image)
    project(mod(mate + 2, NX))
    bundle(xo, 3)
    project(xo)
    attend(1 - image)

    store_att = pltpu.make_async_copy(att_ref, att_hbm, sem_att)
    store_att.start()

    def grad_tile(t):
        u = mod(t, 4)
        d_all = dqkv[...].reshape(GROUP, QKV)
        for hh in range(NH):
            cols = pl.ds(pl.multiple_of((u + 4 * hh) * TILE, 128), TILE)
            tile = normed[:, :, :, :, cols].reshape(GROUP, TILE)
            grads[hh, pl.ds(4 * u, 4)] = dot(tile, d_all, 0, 0).astype(BF16).reshape(4, OWN, QKV)

    def z_part(s, sub, part, right):
        zz = mod(z + 8 - s + NZ, NZ) if right else mod(z + 9 + s, NZ)
        came, sem, device = (zin_r, sem_zr, to_zr) if right else (zin_l, sem_zl, to_zl)
        rows = pl.ds(part * PART, PART)
        block = grads.at[(other_h, h)[sub], zz, rows]
        if s > 0:
            arrived(came.at[s - 1, sub, rows], sem.at[s - 1, sub * Z_PARTS + part])
            block[...] = (block[...].astype(F32) + came[s - 1, sub, rows].astype(F32)).astype(BF16)
        last = s == (RIGHT_STEPS if right else LEFT_STEPS) - 1
        if last and sub == 0:
            slot = 1 if right else 2
            send(block, yh_in.at[slot, rows], out_z, sem_yh.at[slot, part], over_zr if right else over_zl)
        else:
            send(block, came.at[s, sub, rows], out_z, sem.at[s, sub * Z_PARTS + part], device)

    def z_step(s, ways=(True, False)):
        for sub in range(2):
            for part in range(Z_PARTS):
                for right in ways:
                    if right or s < LEFT_STEPS:
                        z_part(s, sub, part, right)

    def own_over():
        block = grads.at[other_h, z]
        send(block, yh_in.at[0], out_z, sem_own, over)

    def share(j, carry):
        cols = pl.ds(pl.multiple_of(j * 256, 256), 256)
        out = dot(dqkv[...].reshape(GROUP, QKV), w[cols, :], 1, 1).astype(BF16)
        terms[:, :, :, :, cols] = out.reshape(NX, NY, NC, ROWS, 256)
        return carry

    order = (xo, xr, xl, x)
    ys = [mod(y + 1, NY), mod(y + 2, NY), mod(y + 3, NY), y]

    def both_cores(j, k):
        return terms[order[j], ys[k], c].astype(F32) + from_core[j, ys[k]].astype(F32)

    def start_x(k):
        block = terms.at[xo, ys[k], c]
        block[...] = both_cores(0, k).astype(BF16)
        send(block.at[:, pl.ds(0, HALF)], half_l.at[k], out_mp, sem_hl.at[k], to_right)
        send(block.at[:, pl.ds(HALF, HALF)], half_r.at[k], out_mp, sem_hr.at[k], to_left)

    def relay_x(k):
        total = both_cores(1, k)
        block = terms.at[xr, ys[k], c]
        arrived(half_l.at[k], sem_hl.at[k])
        block[:, :HALF] = (total[:, :HALF] + half_l[k].astype(F32)).astype(BF16)
        block[:, HALF:] = total[:, HALF:].astype(BF16)
        send(block, full_l.at[k], out_mp, sem_fl.at[k], to_right)
        total = both_cores(2, k)
        block = terms.at[xl, ys[k], c]
        arrived(half_r.at[k], sem_hr.at[k])
        block[:, :HALF] = total[:, :HALF].astype(BF16)
        block[:, HALF:] = (total[:, HALF:] + half_r[k].astype(F32)).astype(BF16)
        send(block, full_r.at[k], out_mp, sem_fr.at[k], to_left)

    def end_x(k):
        total = both_cores(3, k)
        arrived(full_l.at[k], sem_fl.at[k])
        arrived(full_r.at[k], sem_fr.at[k])
        total = total + full_l[k].astype(F32) + full_r[k].astype(F32)
        if k == NY - 1:
            return total
        block = terms.at[x, ys[k], c]
        block[...] = total.astype(BF16)
        send(block, from_y.at[y], out_mp, sem_fy.at[y], at_mp(x, ys[k], c))
        return None

    first = div(mod(z + 8, NZ), 4)
    grad_tile(first)
    z_step(0, (True,))
    grad_tile(first + 1)
    z_step(0, (False,))
    lax.fori_loop(0, D // 256, share, 0)
    for j in range(NX):
        send(terms.at[order[j], :, other_c], from_core.at[j], out_mp, sem_core.at[j], to_sib)
    grad_tile(first + 3)
    z_step(1)
    arrived(from_core.at[0], sem_core.at[0])
    for k in range(NY):
        start_x(k)
    grad_tile(first + 2)
    own_over()
    z_step(2)
    arrived(from_core.at[1], sem_core.at[1])
    arrived(from_core.at[2], sem_core.at[2])
    relay_x(0)
    relay_x(1)
    z_step(3)
    relay_x(2)
    relay_x(3)
    z_step(4)
    arrived(from_core.at[3], sem_core.at[3])
    end_x(0)
    z_step(5)
    end_x(1)
    end_x(2)
    z_step(6)
    d_normed = end_x(3)
    z_step(7)
    for k in range(NY - 1):
        arrived(from_y.at[ys[k]], sem_fy.at[ys[k]])
        d_normed = d_normed + from_y[ys[k]].astype(F32)
    rows = in_ref[...].astype(F32)
    centered = rows - jnp.sum(rows, -1, keepdims=True) * (1.0 / D)
    inv = lax.rsqrt(jnp.sum(centered * centered, -1, keepdims=True) * (1.0 / D) + 1e-6)
    hat = centered * inv
    grown = d_normed * gain_ref[...]
    lean = jnp.sum(grown * hat, -1, keepdims=True) * (1.0 / D)
    ing_ref[...] = (inv * (grown - jnp.sum(grown, -1, keepdims=True) * (1.0 / D) - hat * lean)).astype(BF16)
    store_ing = pltpu.make_async_copy(ing_ref, ing_hbm, sem_ing)
    store_ing.start()

    total = grads[h, z].astype(F32)
    arrived(yh_in.at[0], sem_own)
    total = total + yh_in[0].astype(F32)
    for part in range(Z_PARTS):
        rows = pl.ds(part * PART, PART)
        arrived(zin_l.at[LEFT_STEPS - 1, 1, rows], sem_zl.at[LEFT_STEPS - 1, Z_PARTS + part])
        arrived(yh_in.at[2, rows], sem_yh.at[2, part])
    total = total + zin_l[LEFT_STEPS - 1, 1].astype(F32) + yh_in[2].astype(F32)
    for part in range(Z_PARTS):
        rows = pl.ds(part * PART, PART)
        arrived(zin_r.at[RIGHT_STEPS - 1, 1, rows], sem_zr.at[RIGHT_STEPS - 1, Z_PARTS + part])
        arrived(yh_in.at[1, rows], sem_yh.at[1, part])
    total = total + zin_r[RIGHT_STEPS - 1, 1].astype(F32) + yh_in[1].astype(F32)
    wg_ref[...] = total.reshape(OWN, 1, QKV)
    store_wg = pltpu.make_async_copy(wg_ref, wg_hbm, sem_wg)
    store_wg.start()

    for sem in (out_ag, out_mp):
        arrived(normed.at[pl.ds(0, 3)], sem)
        arrived(normed.at[3, pl.ds(0, 3)], sem)
        arrived(normed.at[3, 3, 0], sem)
    arrived(grads.at[0], out_z)
    arrived(grads.at[1, pl.ds(0, 15)], out_z)
    store_att.wait()
    store_ing.wait()
    store_wg.wait()


def local(inputs, gain, qkv_weight, d_attended):
    anywhere = pl.BlockSpec(memory_space=pl.ANY)
    dma = pltpu.SemaphoreType.DMA
    blocks = (NX, NY, NC, ROWS, D)
    attended, input_grad, weight_grad = pl.pallas_call(
        kernel,
        out_shape=(
            jax.ShapeDtypeStruct((2, IMAGE, HD), BF16),
            jax.ShapeDtypeStruct((ROWS, D), BF16),
            jax.ShapeDtypeStruct((OWN, 1, QKV), F32),
        ),
        in_specs=[anywhere] * 4,
        out_specs=(anywhere,) * 3,
        scratch_shapes=[
            pltpu.VMEM((2, IMAGE, HD), BF16),
            pltpu.VMEM((ROWS, D), BF16),
            pltpu.VMEM((OWN, 1, QKV), F32),
            pltpu.VMEM((ROWS, D), BF16),
            pltpu.VMEM((1, D), F32),
            pltpu.VMEM((D, QKV), BF16),
            pltpu.VMEM((2, IMAGE, HD), BF16),
            pltpu.VMEM(blocks, BF16),
            pltpu.VMEM((NX, IMAGE // 2, QKV), BF16),
            pltpu.VMEM((2, IMAGE, QKV), BF16),
            pltpu.VMEM((NH, NZ, OWN, QKV), BF16),
            pltpu.VMEM(blocks, BF16),
            pltpu.VMEM((NX, NY, ROWS, D), BF16),
            pltpu.VMEM((NY, ROWS, HALF), BF16),
            pltpu.VMEM((NY, ROWS, HALF), BF16),
            pltpu.VMEM((NY, ROWS, D), BF16),
            pltpu.VMEM((NY, ROWS, D), BF16),
            pltpu.VMEM((NY, ROWS, D), BF16),
            pltpu.VMEM((RIGHT_STEPS, 2, OWN, QKV), BF16),
            pltpu.VMEM((LEFT_STEPS, 2, OWN, QKV), BF16),
            pltpu.VMEM((3, OWN, QKV), BF16),
            dma, dma, dma, dma,
            dma((NY,)), dma((NY, 2)), dma((NY, 2)), dma((NY,)), dma((NY,)), dma((NY,)), dma((4,)),
            dma((RIGHT_STEPS, 2 * Z_PARTS)), dma((LEFT_STEPS, 2 * Z_PARTS)),
            dma((NX,)), dma((NY,)), dma((NY,)), dma((NY,)), dma((NY,)), dma((NY,)), dma((3, Z_PARTS)), dma, dma, dma, dma,
            dma, dma, dma,
        ],
        compiler_params=pltpu.CompilerParams(
            collective_id=0, has_side_effects=True, vmem_limit_bytes=60 * 1024 * 1024
        ),
    )(inputs, gain.reshape(1, D), qkv_weight.reshape(D, QKV), d_attended.reshape(2, IMAGE, HD))
    return (attended.reshape(GROUP, 1, HD), input_grad, weight_grad)


def solution(mesh):
    return jax.shard_map(
        local,
        mesh=mesh,
        in_specs=(P(("dp", "mp"), None), P(), P(None, "mp", None), P("dp", "mp", None)),
        out_specs=(P("dp", "mp", None), P(("dp", "mp"), None), P("dp", "mp", None)),
        check_vma=False,
    )
```

time: 91.6 us -> 85.7 us (0.936)
  the two profiles are of different devices: /device:TPU:56 before, /device:TPU:8 now
where the time goes in v2:
time: 85.7 us; the launch traced here: 85.5 us
  Pallas kernels  80.1 us (93%)
  local copies, waits for them, and re-layouts  4.74 us (6%)
    pallas_call x1, Pallas kernels, local(): pl.pallas_call(kernel, out_shape=(jax.ShapeDtypeStruct((2, IMAGE, HD), BF...  80.1 us
    unnamed x3, local copies, waits for them, and re-layouts  4.74 us

profile of v2, /device:TPU:8, one launch (start us, length us, event | category | flops | bytes accessed | tf_op | source)
XLA Modules:
  0.0 85.5 jit_solution(6063750693449439612)
XLA Ops:
  0.6 80.1 %shard_map.67 = (bf16[2,256,128]{2,1,0:T(8,128)(2,1)}, bf16[16,3072]{1,0:T(8,128)(2,1)}, f32[96,1,384]{2,1,0:T(1,128)}) custom-call(bf16[16,3072]{1,0:T(8,128)(2,1)} %in_hbm.1, f32[1,3072]{1,0:T(1,128)} %bitcast.7, bf16[3072,384]{1,0:T(8,128)(2,1)} %bitcast.4, bf16[2,256,128]{2,1,0:T(8,128)(2,1)} %bitcast.5), custom_call_target="tpu_custom_call" | custom-call | tf_op jit(solution)/shard_map/pallas_call | solution.py:365
  80.7 1.6 %copy.10 = bf16[512,1,128]{2,0,1:T(8,128)(2,1)} copy(bf16[512,1,128]{2,0,1:T(8,128)(2,1)} %bitcast.6) | data formatting | bytes 262144
  82.3 1.5 %copy.11 = bf16[16,3072]{1,0:T(8,128)(2,1)} copy(bf16[16,3072]{1,0:T(8,128)(2,1)} %get-tuple-element.13) | data formatting | bytes 196608
  83.8 1.6 %copy.12 = f32[96,1,384]{2,1,0:T(1,128)} copy(f32[96,1,384]{2,1,0:T(1,128)} %get-tuple-element.14) | data formatting | bytes 294912

commit v3 on v2

--- a/solution.py
+++ b/solution.py
@@ -7,7 +7,7 @@
 
 MESH = pl.DeviceIdType.MESH
 STRAIGHT = (True, False, False, True)
-Y_FIRST = (1, 2, 3)
+FAR_AT = 1
 Z_PARTS = 2
 BF16, F32 = jnp.bfloat16, jnp.float32
 
@@ -41,12 +41,11 @@
 
 def kernel(
     in_hbm, gain_hbm, w_hbm, do_hbm,
-    att_hbm, ing_hbm, wg_hbm,
     att_ref, ing_ref, wg_ref,
     in_ref, gain_ref, w, do, normed, qkv, dqkv, grads, terms, from_core, half_l, half_r, full_l, full_r, from_y,
     zin_r, zin_l, yh_in,
     sem_in, sem_gain, sem_w, sem_do, sem_y, sem_xl, sem_xr, sem_xo, sem_x2l, sem_x2r, sem_sib,
-    sem_zr, sem_zl, sem_core, sem_hl, sem_hr, sem_fl, sem_fr, sem_fy, sem_yh, sem_own, sem_att, sem_ing, sem_wg,
+    sem_zr, sem_zl, sem_core, sem_hl, sem_hr, sem_fl, sem_fr, sem_fy, sem_yh, sem_own,
     out_ag, out_z, out_mp,
 ):
     dp, mp = lax.axis_index("dp"), lax.axis_index("mp")
@@ -55,6 +54,9 @@
     xr, xl, xo = mod(x + 1, NX), mod(x + 3, NX), mod(x + 2, NX)
     other_c, other_h = 1 - c, 1 - h
     near = [y, y + 1 - 2 * mod(y, 2), mod(y + 2, NY), NY - 1 - y]
+    middle = div(mod(y + 1, NY), 2)
+    swap = middle * (near[3] - near[2])
+    near[2], near[3] = near[2] + swap, near[3] - swap
 
     def at_mp(xx, yy, cc):
         return (dp, xx * 8 + yy * 2 + cc)
@@ -105,11 +107,20 @@
             part = block.at[:, pieces[p]]
             sem, device = (sem_xl, to_right) if right else (sem_xr, to_left)
             send(part, part, out_ag, sem.at[yy, p], device)
-        if STRAIGHT[k]:
+        if k == 0:
             send(block, block, out_ag, sem_xo.at[yy], to_across)
 
     def along_y(k):
         send(own, own, out_ag, sem_y.at[y], at_mp(x, near[k], c))
+
+    def past_middle():
+        block = normed.at[x, near[2], c]
+        send(block, block, out_ag, sem_y.at[near[2]], at_mp(x, near[1], c))
+
+    def far_across():
+        block = normed.at[xo, y, c]
+        send(block, block, out_ag, sem_xo.at[y], at_mp(x, NY - 1 - y, c))
+        send(block, block, out_ag, sem_xo.at[y], at_mp(x, mod(y + 2, NY), c))
 
     def pass_on(k):
         yy = near[k]
@@ -130,26 +141,6 @@
         to_sibling(normed.at[xl, yy, c], 1)
         arrived(normed.at[xr, yy, c, :, pieces[0]], sem_xr.at[yy, 0])
         to_sibling(normed.at[xr, yy, c], 2)
-
-    own = normed.at[x, y, c]
-    along_x(0)
-    for k in Y_FIRST:
-        along_y(k)
-    to_sibling(own, 0)
-    for k in range(NY):
-        if k + 1 < NY:
-            yy = near[k + 1]
-            arrived(normed.at[x, yy, c], sem_y.at[yy])
-            along_x(k + 1)
-            to_sibling(normed.at[x, yy, c], 0)
-        if k == 0:
-            for j in (1, 2, 3):
-                if j not in Y_FIRST:
-                    along_y(j)
-        pass_on(k)
-        if k > 0:
-            finish_x(k - 1)
-    finish_x(NY - 1)
 
     def second(k):
         yy = near[k]
@@ -162,6 +153,27 @@
             part = normed.at[xo, yy, c, :, pieces[p]]
             arrived(part, sem.at[yy])
             to_sibling(part, 3)
+
+    own = normed.at[x, y, c]
+    along_y(1)
+    along_y(2)
+    along_x(0)
+    pl.when(middle == 0)(lambda: along_y(3))
+    to_sibling(own, 0)
+    for k in range(NY):
+        if k + 1 < NY:
+            yy = near[k + 1]
+            arrived(normed.at[x, yy, c], sem_y.at[yy])
+            if k + 1 == 2:
+                pl.when(middle == 1)(past_middle)
+            along_x(k + 1)
+            to_sibling(normed.at[x, yy, c], 0)
+        pass_on(k)
+        if k > 0:
+            finish_x(k - 1)
+        if k == FAR_AT:
+            second(0)
+            pl.when(middle == 0)(far_across)
 
     def bundle(xx, slot):
         arrived(normed.at[xx, :, other_c], sem_sib.at[slot])
@@ -185,27 +197,24 @@
         dqkv[a, :, :HD] = dot(d_scores, k, 1, 0).astype(BF16)
         dqkv[a, :, HD : 2 * HD] = dot(d_scores, q, 0, 0).astype(BF16)
 
+    image = div(x, 2)
+    mate = x + 1 - 2 * mod(x, 2)
     load_w.wait()
     load_do.wait()
     bundle(x, 0)
     project(x)
-    second(0)
+    finish_x(NY - 1)
     second(1)
+    second(2)
     bundle(xl, 1)
     bundle(xr, 2)
-    image = div(x, 2)
-    mate = x + 1 - 2 * mod(x, 2)
     project(mate)
-    second(2)
+    project(mod(mate + 2, NX))
     second(3)
     attend(image)
-    project(mod(mate + 2, NX))
     bundle(xo, 3)
     project(xo)
     attend(1 - image)
-
-    store_att = pltpu.make_async_copy(att_ref, att_hbm, sem_att)
-    store_att.start()
 
     def grad_tile(t):
         u = mod(t, 4)
@@ -327,8 +336,6 @@
     grown = d_normed * gain_ref[...]
     lean = jnp.sum(grown * hat, -1, keepdims=True) * (1.0 / D)
     ing_ref[...] = (inv * (grown - jnp.sum(grown, -1, keepdims=True) * (1.0 / D) - hat * lean)).astype(BF16)
-    store_ing = pltpu.make_async_copy(ing_ref, ing_hbm, sem_ing)
-    store_ing.start()
 
     total = grads[h, z].astype(F32)
     arrived(yh_in.at[0], sem_own)
@@ -344,18 +351,15 @@
         arrived(yh_in.at[1, rows], sem_yh.at[1, part])
     total = total + zin_r[RIGHT_STEPS - 1, 1].astype(F32) + yh_in[1].astype(F32)
     wg_ref[...] = total.reshape(OWN, 1, QKV)
-    store_wg = pltpu.make_async_copy(wg_ref, wg_hbm, sem_wg)
-    store_wg.start()
-
-    for sem in (out_ag, out_mp):
-        arrived(normed.at[pl.ds(0, 3)], sem)
-        arrived(normed.at[3, pl.ds(0, 3)], sem)
-        arrived(normed.at[3, 3, 0], sem)
+
+    arrived(normed.at[pl.ds(0, 3)], out_mp)
+    arrived(normed.at[3, pl.ds(0, 3)], out_mp)
+    arrived(normed.at[3, 3, 0], out_mp)
+    arrived(normed.at[pl.ds(0, 3)], out_ag)
+    arrived(normed.at[3, pl.ds(0, 3)], out_ag)
+    pl.when(middle == 0)(lambda: arrived(normed.at[3, 3], out_ag))
     arrived(grads.at[0], out_z)
     arrived(grads.at[1, pl.ds(0, 15)], out_z)
-    store_att.wait()
-    store_ing.wait()
-    store_wg.wait()
 
 
 def local(inputs, gain, qkv_weight, d_attended):
@@ -365,16 +369,13 @@
     attended, input_grad, weight_grad = pl.pallas_call(
         kernel,
         out_shape=(
-            jax.ShapeDtypeStruct((2, IMAGE, HD), BF16),
-            jax.ShapeDtypeStruct((ROWS, D), BF16),
-            jax.ShapeDtypeStruct((OWN, 1, QKV), F32),
-        ),
-        in_specs=[anywhere] * 4,
-        out_specs=(anywhere,) * 3,
-        scratch_shapes=[
             pltpu.VMEM((2, IMAGE, HD), BF16),
             pltpu.VMEM((ROWS, D), BF16),
             pltpu.VMEM((OWN, 1, QKV), F32),
+        ),
+        in_specs=[pl.BlockSpec(memory_space=pltpu.HBM)] * 4,
+        out_specs=(pl.BlockSpec(memory_space=pltpu.VMEM),) * 3,
+        scratch_shapes=[
             pltpu.VMEM((ROWS, D), BF16),
             pltpu.VMEM((1, D), F32),
             pltpu.VMEM((D, QKV), BF16),
@@ -396,7 +397,7 @@
             dma, dma, dma, dma,
             dma((NY,)), dma((NY, 2)), dma((NY, 2)), dma((NY,)), dma((NY,)), dma((NY,)), dma((4,)),
             dma((RIGHT_STEPS, 2 * Z_PARTS)), dma((LEFT_STEPS, 2 * Z_PARTS)),
-            dma((NX,)), dma((NY,)), dma((NY,)), dma((NY,)), dma((NY,)), dma((NY,)), dma((3, Z_PARTS)), dma, dma, dma, dma,
+            dma((NX,)), dma((NY,)), dma((NY,)), dma((NY,)), dma((NY,)), dma((NY,)), dma((3, Z_PARTS)), dma,
             dma, dma, dma,
         ],
         compiler_params=pltpu.CompilerParams(

time: 85.7 us -> 80.7 us (0.942)
  local copies, waits for them, and re-layouts: 4.74 us -> 1.96 us
  Pallas kernels: 80.1 us -> 78 us
    unnamed x3, local copies, waits for them, and re-layouts: 4.74 us -> 1.96 us
    pallas_call x1, Pallas kernels: 80.1 us -> 78 us  [local(): pl.pallas_call(kernel, out_shape=(pltpu.VMEM((2, IMAGE, HD), BF16), pltpu...]
where the time goes in v3:
time: 80.7 us; the launch traced here: 80.6 us
  Pallas kernels  78 us (97%)
  local copies, waits for them, and re-layouts  1.96 us (2%)
    pallas_call x1, Pallas kernels, local(): pl.pallas_call(kernel, out_shape=(pltpu.VMEM((2, IMAGE, HD), BF16), pltpu...  78 us
    unnamed x3, local copies, waits for them, and re-layouts  1.96 us

profile of v3, /device:TPU:8, one launch (start us, length us, event | category | flops | bytes accessed | tf_op | source)
XLA Modules:
  0.0 80.6 jit_solution(4054640933937202902)
XLA Ops:
  0.6 78.0 %shard_map.67 = (bf16[2,256,128]{2,1,0:T(8,128)(2,1)S(1)}, bf16[16,3072]{1,0:T(8,128)(2,1)S(1)}, f32[96,1,384]{2,1,0:T(1,128)S(1)}) custom-call(bf16[16,3072]{1,0:T(8,128)(2,1)} %in_hbm.1, f32[1,3072]{1,0:T(1,128)} %bitcast.7, bf16[3072,384]{1,0:T(8,128)(2,1)} %bitcast.5, bf16[2,256,128]{2,1,0:T(8,128)(2,1)} %bitcast.6), custom_call_target="tpu_custom_call" | custom-call | tf_op jit(solution)/shard_map/pallas_call | solution.py:369
  78.6 0.7 copy.10
  79.3 0.6 copy.11
  79.9 0.7 copy.12

commit v4 on v3

--- a/solution.py
+++ b/solution.py
@@ -239,21 +239,24 @@
         else:
             send(block, came.at[s, sub, rows], out_z, sem.at[s, sub * Z_PARTS + part], device)
 
-    def z_step(s, ways=(True, False)):
+    def z_step(s, ways):
         for sub in range(2):
-            for part in range(Z_PARTS):
-                for right in ways:
-                    if right or s < LEFT_STEPS:
-                        z_part(s, sub, part, right)
+            z_half(s, sub, ways)
+
+    def z_half(s, sub, ways=(True, False)):
+        for part in range(Z_PARTS):
+            for right in ways:
+                if right or s < LEFT_STEPS:
+                    z_part(s, sub, part, right)
 
     def own_over():
         block = grads.at[other_h, z]
         send(block, yh_in.at[0], out_z, sem_own, over)
 
     def share(j, carry):
-        cols = pl.ds(pl.multiple_of(j * 256, 256), 256)
+        cols = pl.ds(j * 512, 512)
         out = dot(dqkv[...].reshape(GROUP, QKV), w[cols, :], 1, 1).astype(BF16)
-        terms[:, :, :, :, cols] = out.reshape(NX, NY, NC, ROWS, 256)
+        terms[:, :, :, :, cols] = out.reshape(NX, NY, NC, ROWS, 512)
         return carry
 
     order = (xo, xr, xl, x)
@@ -299,33 +302,43 @@
     z_step(0, (True,))
     grad_tile(first + 1)
     z_step(0, (False,))
-    lax.fori_loop(0, D // 256, share, 0)
+    for j in range(D // 512):
+        share(j, 0)
     for j in range(NX):
         send(terms.at[order[j], :, other_c], from_core.at[j], out_mp, sem_core.at[j], to_sib)
     grad_tile(first + 3)
-    z_step(1)
+    z_half(1, 0)
     arrived(from_core.at[0], sem_core.at[0])
-    for k in range(NY):
-        start_x(k)
+    start_x(0)
+    start_x(1)
+    z_half(1, 1)
+    start_x(2)
+    start_x(3)
+    z_half(2, 0)
     grad_tile(first + 2)
     own_over()
-    z_step(2)
+    z_half(2, 1)
     arrived(from_core.at[1], sem_core.at[1])
     arrived(from_core.at[2], sem_core.at[2])
     relay_x(0)
     relay_x(1)
-    z_step(3)
+    z_half(3, 0)
     relay_x(2)
+    z_half(3, 1)
     relay_x(3)
-    z_step(4)
     arrived(from_core.at[3], sem_core.at[3])
+    z_half(4, 0)
+    z_half(4, 1)
     end_x(0)
-    z_step(5)
+    z_half(5, 0)
     end_x(1)
+    z_half(5, 1)
     end_x(2)
-    z_step(6)
+    z_half(6, 0)
+    z_half(6, 1)
     d_normed = end_x(3)
-    z_step(7)
+    z_half(7, 0)
+    z_half(7, 1)
     for k in range(NY - 1):
         arrived(from_y.at[ys[k]], sem_fy.at[ys[k]])
         d_normed = d_normed + from_y[ys[k]].astype(F32)

time: 80.7 us -> 79 us (0.979)
  Pallas kernels: 78 us -> 76.2 us
    pallas_call x1, Pallas kernels: 78 us -> 76.2 us  [local(): pl.pallas_call(kernel, out_shape=(pltpu.VMEM((2, IMAGE, HD), BF16), pltpu...]
where the time goes in v4:
time: 79 us; the launch traced here: 78.8 us
  Pallas kernels  76.2 us (96%)
  local copies, waits for them, and re-layouts  1.96 us (2%)
    pallas_call x1, Pallas kernels, local(): pl.pallas_call(kernel, out_shape=(pltpu.VMEM((2, IMAGE, HD), BF16), pltpu...  76.2 us
    unnamed x3, local copies, waits for them, and re-layouts  1.96 us

profile of v4, /device:TPU:8, one launch (start us, length us, event | category | flops | bytes accessed | tf_op | source)
XLA Modules:
  0.0 78.8 jit_solution(16047655393441412143)
XLA Ops:
  0.6 76.2 %shard_map.67 = (bf16[2,256,128]{2,1,0:T(8,128)(2,1)S(1)}, bf16[16,3072]{1,0:T(8,128)(2,1)S(1)}, f32[96,1,384]{2,1,0:T(1,128)S(1)}) custom-call(bf16[16,3072]{1,0:T(8,128)(2,1)} %in_hbm.1, f32[1,3072]{1,0:T(1,128)} %bitcast.7, bf16[3072,384]{1,0:T(8,128)(2,1)} %bitcast.5, bf16[2,256,128]{2,1,0:T(8,128)(2,1)} %bitcast.6), custom_call_target="tpu_custom_call" | custom-call | tf_op jit(solution)/shard_map/pallas_call | solution.py:382
  76.9 0.7 copy.10
  77.5 0.6 copy.11
  78.2 0.7 copy.12
